TPU v7x, 512 devices: a whole 4x8x8 slice. The times are simulated.
512 devices in a mesh: leaf: 256 (over x, z, y), tile: 2 (over core).
Axes of the slice: x: 4, y: 8, z: 8, core: 2. Of those that a mesh axis runs over, the one named last changes fastest.
Arguments:
- margin_diag: float32 [65536, 256], P('leaf', 'tile'), may hold values from -0.05 to 1.05, as said below
- coupling_near: float32 [65536, 256], P('leaf', 'tile'), may hold values from -0.07 to 0.07
- coupling_far: float32 [65536, 256], P('leaf', 'tile'), may hold values from -0.07 to 0.07
- leaf_factor: float32 [65536, 256], P('leaf', 'tile')
- tile_rows: int32 [256, 2, 4], P('leaf'), may hold values from 0 to 255, as said below
- tile_counts: int32 [256, 2], P('leaf'), may hold values from 1 to 4, as said below
Outputs:
- factor: float32 [1024, 65536], P(None, ('leaf', 'tile'))
Inputs may be any that keep to these rules, and one draw needn't show every extreme that they name: Each row block of margin_diag is a symmetric 256 x 256 tile, as an margin tile is. `tile_rows`: every entry names a leaf of the column leaf's group of four. Entry 0 of each list is the leaf itself; at level 0 entry 1 is its sibling i XOR a, and further entries are padding; at level 1 entries 1 to 3 are the other three group members in some order. Entries past the count are padding. `tile_counts`: level 0 counts are 1 or 2, level 1 counts 1 to 4; in every draw some leaf has a full list at each level.
All inputs are finite; a program needn't handle non-finite values.
Results may differ from a plain program's by a relative error of at most 0.0003.
Values sent between devices are 32-bit elements; how exact they have to be, the bound alone decides.
A program may use at most 64 MiB of HBM per device.

v0:
```python
import functools

import jax
import jax.numpy as jnp
from jax import lax
from jax.experimental import pallas as pl
from jax.experimental.pallas import tpu as pltpu

MESH = pl.DeviceIdType.MESH
T = 256
H = 128
F32 = jnp.float32
BF16 = jnp.bfloat16


def split(x):
    high = x.astype(BF16)
    return high, (x - high.astype(F32)).astype(BF16)


def nn(a, b):
    return lax.dot_general(a, b, (((1,), (0,)), ((), ())), preferred_element_type=F32)


def nt(a, b):
    return lax.dot_general(a, b, (((1,), (1,)), ((), ())), preferred_element_type=F32)


def mm(a, b, dot=nn):
    rows = a[0].shape[0]
    if rows <= 128:
        both = dot(jnp.concatenate([a[0], a[1]], 0), b[0])
        return both[:rows] + (both[rows:] + dot(a[0], b[1]))
    return dot(a[0], b[0]) + (dot(a[0], b[1]) + dot(a[1], b[0]))


def put(pair_ref, index, value):
    high, low = split(value)
    pair_ref[(0,) + index] = high
    pair_ref[(1,) + index] = low


def get(pair_ref, index):
    return pair_ref[(0,) + index], pair_ref[(1,) + index]


ALL = slice(None)


def tl(k):
    return slice(k * T, (k + 1) * T)


def eye(offset, rows):
    row = lax.broadcasted_iota(jnp.int32, (rows, T), 0) + offset
    col = lax.broadcasted_iota(jnp.int32, (rows, T), 1)
    return jnp.where(row == col, 1.0, 0.0).astype(F32)


def kernel(
    stride,
    diag_ref, near_ref, far_ref, leaf_ref, rows_ref, counts_ref,
    out_ref,
    raw, uraw, masks, mown,
    ut, a_mat, far_s, p_mat, v_mat, f_mat, f_cross,
    xs, xr, ms, mr, ds, dr,
):
    leaf = lax.axis_index("leaf")
    core = lax.axis_index("tile")
    pos = leaf // stride
    rest = leaf % stride
    pos1 = pos + 1 - 2 * (pos % 2)
    pos2 = (pos + 2) % 4
    pos3 = 3 - pos
    spot = (pos, pos1, pos2, pos3)
    dev1 = (pos1 * stride + rest, core)
    dev2 = (pos2 * stride + rest, core)
    dev3 = (pos3 * stride + rest, core)
    mate = (leaf, 1 - core)
    half = core * H

    raw[0, 0, core] = diag_ref[...]
    raw[1, 0, core] = near_ref[...]
    raw[2, 0, core] = far_ref[...]
    uraw[0, core] = leaf_ref[...].T
    for level in range(2):
        for s in range(4):
            hit = jnp.float32(0.0)
            for e in range(4):
                value = rows_ref[0, level, e]
                place = 2 * (value // (2 * stride) % 2) + value // stride % 2
                live = jnp.logical_and(e < counts_ref[0, level], place == spot[s])
                hit = jnp.where(live, jnp.float32(1.0), hit)
            mown[pl.ds(level * 4 + s, 1), :] = jnp.full((1, 128), hit, F32)

    barrier = pltpu.get_barrier_semaphore()
    for device in (dev1, dev2, dev3, mate):
        pl.semaphore_signal(barrier, inc=1, device_id=device, device_id_type=MESH)
    pl.semaphore_wait(barrier, 4)

    def tile_ref(kind, slot, side, piece):
        if kind == 3:
            if piece is None:
                return uraw.at[slot, side]
            return uraw.at[slot, side, pl.ds(piece * 64, 64)]
        if piece is None:
            return raw.at[kind, slot, side]
        return raw.at[kind, slot, side, pl.ds(piece * H, H)]

    def to_chip(kind, src_slot, piece, dst_slot, device, sem):
        return pltpu.make_async_remote_copy(
            src_ref=tile_ref(kind, src_slot, core, piece),
            dst_ref=tile_ref(kind, dst_slot, core, piece),
            send_sem=xs.at[kind, sem], recv_sem=xr.at[kind, sem],
            device_id=device, device_id_type=MESH,
        )

    def to_mate(kind, slot, piece, sem):
        return pltpu.make_async_remote_copy(
            src_ref=tile_ref(kind, slot, core, piece),
            dst_ref=tile_ref(kind, slot, core, piece),
            send_sem=ds.at[kind, sem], recv_sem=dr.at[kind, sem],
            device_id=mate, device_id_type=MESH,
        )

    def own1(kind):
        return to_chip(kind, 0, None, 1, dev1, 0)

    def own3(kind):
        return to_chip(kind, 0, None, 3, dev3, 1)

    def fwd1(kind):
        return to_chip(kind, 3, 0, 2, dev1, 2)

    def fwd3(kind):
        return to_chip(kind, 1, 1, 2, dev3, 3)

    def masks_to(slot, device):
        return pltpu.make_async_remote_copy(
            src_ref=mown, dst_ref=masks.at[slot],
            send_sem=ms.at[slot], recv_sem=mr.at[slot],
            device_id=device, device_id_type=MESH,
        )

    mask_copies = [masks_to(1, dev1), masks_to(2, dev2), masks_to(3, dev3)]
    for copy in mask_copies:
        copy.start()
    for kind in (1, 3, 0):
        own1(kind).start()
        own3(kind).start()
    for kind in (3, 0, 1, 2):
        to_mate(kind, 0, None, 0).start()

    def hop(kind):
        own1(kind).wait_recv()
        to_mate(kind, 1, None, 1).start()
        fwd3(kind).start()
        own3(kind).wait_recv()
        to_mate(kind, 3, None, 3).start()
        fwd1(kind).start()

    def hop2(kind):
        fwd1(kind).wait_recv()
        to_mate(kind, 2, 0, 2).start()
        fwd3(kind).wait_recv()
        to_mate(kind, 2, 1, 4).start()

    def mate_in(kind, slot):
        if slot == 2:
            to_mate(kind, 2, 0, 2).wait_recv()
            to_mate(kind, 2, 1, 4).wait_recv()
        else:
            to_mate(kind, slot, None, slot).wait_recv()

    for kind in (1, 3, 0):
        hop(kind)
    own1(2).start()
    own3(2).start()

    for copy in mask_copies:
        copy.wait_recv()
    masks[0] = mown[...]

    def mask(level, column, row):
        line = masks[column, pl.ds(level * 4 + (column ^ row), 1), :]
        return jnp.concatenate([line, line], axis=1)

    def whole(kind, slot):
        return jnp.concatenate([raw[kind, slot, 0], raw[kind, slot, 1]], axis=1)

    def pair(g):
        s0, s1 = 2 * g, 2 * g + 1
        for k, slot in enumerate((s0, s1)):
            put(a_mat, (g, tl(k), tl(k)), whole(0, slot))
            put(ut, (slot,), jnp.concatenate([uraw[slot, 0], uraw[slot, 1]], axis=0))
        first = whole(1, s0)
        second = whole(1, s1)
        cross = 0.5 * (first + second.T)
        put(a_mat, (g, tl(0), tl(1)), cross)
        put(a_mat, (g, tl(1), tl(0)), cross.T)
        one = eye(0, T)
        for j in range(2):
            v = split(mm(get(ut, (2 * g + j,)), get(a_mat, (g, tl(j), ALL))))
            for r in range(2):
                gram = mm((v[0][:, tl(r)], v[1][:, tl(r)]), get(ut, (2 * g + r,)), nt)
                f = -0.5 * gram
                if r == j:
                    f = f + 1.5 * one
                new = mm(split(f), get(ut, (2 * g + r,)))
                new = new * mask(0, 2 * g + j, 2 * g + r)
                put(p_mat, (g, tl(j), tl(r)), new)

        def gram_of():
            put(v_mat, (), mm(get(p_mat, (g,)), get(a_mat, (g,))))
            gram = mm(get(v_mat, ()), get(p_mat, (g,)), nt)
            for j in range(2):
                for r in range(2):
                    f = -0.5 * gram[tl(j), tl(r)]
                    if r == j:
                        f = f + 1.5 * one
                    put(f_mat, (g, tl(j), tl(r)), f)

        gram_of()
        new = mm(get(f_mat, (g,)), get(p_mat, (g,)))
        for j in range(2):
            for r in range(2):
                put(p_mat, (g, tl(j), tl(r)), new[tl(j), tl(r)] * mask(0, 2 * g + j, 2 * g + r))
        gram_of()

    for slot in (0, 1):
        for kind in (0, 1, 3):
            mate_in(kind, slot)
    pair(0)
    for kind in (1, 3, 0):
        hop2(kind)
    hop(2)
    for slot in (2, 3):
        for kind in (0, 1, 3):
            mate_in(kind, slot)
    pair(1)
    hop2(2)
    for slot in range(4):
        mate_in(2, slot)
    for k in range(2):
        put(far_s, (k,), 0.5 * (whole(2, k) + whole(2, k + 2).T))

    for k in range(2):
        put(v_mat, (ALL, tl(k)), mm(get(p_mat, (0, ALL, tl(k))), get(far_s, (k,))))
    put(f_cross, (), -0.5 * mm(get(v_mat, ()), get(p_mat, (1,)), nt))

    mine = pl.ds(pl.multiple_of(half, H), H)
    u0 = mm(get(f_mat, (0, mine, ALL)), get(p_mat, (0,)))
    u1 = mm(get(f_cross, (mine, ALL)), get(p_mat, (1,)))
    u = [u0[:, tl(0)], u0[:, tl(1)], u1[:, tl(0)], u1[:, tl(1)]]
    u = [u[r] * mask(1, 0, r) for r in range(4)]
    us = [split(x) for x in u]

    def beside(parts):
        return tuple(jnp.concatenate([part[i] for part in parts], axis=1) for i in range(2))

    v = []
    for g in range(2):
        vg = mm(beside(us[2 * g:2 * g + 2]), get(a_mat, (g,)))
        for k in range(2):
            extra = mm(us[2 - 2 * g + k], get(far_s, (k,)), nn if g == 1 else nt)
            v.append(split(vg[:, tl(k)] + extra))
    ga = [mm(v[r], get(p_mat, (r // 2, ALL, tl(r % 2))), nt) for r in range(4)]
    terms = [[None] * 4, [None] * 4]
    for l in range(4):
        lhs = []
        for g in range(2):
            m0, m1 = mask(1, l, 2 * g), mask(1, l, 2 * g + 1)
            m0, m1 = jnp.concatenate([m0, m0], 1), jnp.concatenate([m1, m1], 1)
            lhs.append(split(m0 * ga[2 * g] + m1 * ga[2 * g + 1]))
        k = l % 2
        if l < 2:
            gram = mm(lhs[0], get(f_mat, (0, ALL, tl(k)))) + mm(lhs[1], get(f_cross, (tl(k), ALL)), nt)
        else:
            gram = mm(lhs[0], get(f_cross, (ALL, tl(k)))) + mm(lhs[1], get(f_mat, (1, ALL, tl(k))))
        d = -gram
        if l == 0:
            d = d + eye(half, H)
        d = split(d)
        if l < 2:
            terms[0][l] = mm(d, get(f_mat, (0, tl(k), ALL)))
            terms[1][l] = mm(d, get(f_cross, (tl(k), ALL)))
        else:
            terms[0][l] = mm(d, get(f_cross, (ALL, tl(k))), nt)
            terms[1][l] = mm(d, get(f_mat, (1, tl(k), ALL)))
    for r in range(4):
        g, k = r // 2, r % 2
        x = 0.0
        for l in range(4):
            line = mask(1, l, r)
            x = x + jnp.concatenate([line, line], 1) * terms[g][l]
        last = u[r] + 0.5 * mm(split(x), get(p_mat, (g, ALL, tl(k))))
        last = last * mask(1, 0, r)
        out_ref[pl.ds(pl.multiple_of(spot[r] * T, T), T), :] = last.T

    for copy in mask_copies:
        copy.wait_send()
    for kind in range(4):
        for copy in (own1(kind), own3(kind), fwd1(kind), fwd3(kind)):
            copy.wait_send()
        to_mate(kind, 0, None, 0).wait_send()
        to_mate(kind, 1, None, 1).wait_send()
        to_mate(kind, 3, None, 3).wait_send()
        to_mate(kind, 2, 0, 2).wait_send()
        to_mate(kind, 2, 1, 4).wait_send()


def per_device(margin_diag, coupling_near, coupling_far, leaf_factor, tile_rows, tile_counts):
    stride = lax.axis_size("leaf") // 4
    vmem = pl.BlockSpec(memory_space=pltpu.VMEM)
    smem = pl.BlockSpec(memory_space=pltpu.SMEM)
    dma = pltpu.SemaphoreType.DMA
    return pl.pallas_call(
        functools.partial(kernel, stride),
        out_shape=jax.ShapeDtypeStruct((4 * T, H), F32),
        in_specs=[vmem] * 4 + [smem] * 2,
        out_specs=vmem,
        scratch_shapes=[
            pltpu.VMEM((3, 4, 2, T, H), F32),
            pltpu.VMEM((4, 2, H, T), F32),
            pltpu.VMEM((4, 8, 128), F32),
            pltpu.VMEM((8, 128), F32),
            pltpu.VMEM((2, 4, T, T), BF16),
            pltpu.VMEM((2, 2, 2 * T, 2 * T), BF16),
            pltpu.VMEM((2, 2, T, T), BF16),
            pltpu.VMEM((2, 2, 2 * T, 2 * T), BF16),
            pltpu.VMEM((2, 2 * T, 2 * T), BF16),
            pltpu.VMEM((2, 2, 2 * T, 2 * T), BF16),
            pltpu.VMEM((2, 2 * T, 2 * T), BF16),
            dma((4, 4)), dma((4, 4)), dma((4,)), dma((4,)), dma((4, 5)), dma((4, 5)),
        ],
        compiler_params=pltpu.CompilerParams(
            collective_id=0, has_side_effects=True, vmem_limit_bytes=50 * 2**20
        ),
    )(margin_diag, coupling_near, coupling_far, leaf_factor, tile_rows, tile_counts)


def solution(mesh):
    spec = jax.sharding.PartitionSpec
    return jax.shard_map(
        per_device,
        mesh=mesh,
        in_specs=(
            spec("leaf", "tile"),
            spec("leaf", "tile"),
            spec("leaf", "tile"),
            spec("leaf", "tile"),
            spec("leaf", None, None),
            spec("leaf", None),
        ),
        out_specs=spec(None, ("leaf", "tile")),
        check_vma=False,
    )
```

profile of v0, /device:TPU:3, one launch (start us, length us, event | category | flops | bytes accessed | tf_op | source)
XLA Modules:
  0.0 47.3 jit_solution(7906372704336703367)
XLA Ops:
  0.0 0.0 copy-start
  0.0 0.9 %copy-done = f32[256,128]{1,0:T(8,128)S(1)} copy-done((f32[256,128]{1,0:T(8,128)S(1)}, f32[256,128]{1,0:T(8,128)}, u32[]{:S(2)}) %copy-start) | copy-done | bytes 131096
  0.9 0.0 copy-start.1
  0.9 0.9 %copy-done.1 = f32[256,128]{1,0:T(8,128)S(1)} copy-done((f32[256,128]{1,0:T(8,128)S(1)}, f32[256,128]{1,0:T(8,128)}, u32[]{:S(2)}) %copy-start.1) | copy-done | bytes 131096
  1.8 0.0 copy-start.2
  1.8 0.9 %copy-done.2 = f32[256,128]{1,0:T(8,128)S(1)} copy-done((f32[256,128]{1,0:T(8,128)S(1)}, f32[256,128]{1,0:T(8,128)}, u32[]{:S(2)}) %copy-start.2) | copy-done | bytes 131096
  2.7 0.0 copy-start.3
  2.7 0.9 %copy-done.3 = f32[256,128]{1,0:T(8,128)S(1)} copy-done((f32[256,128]{1,0:T(8,128)S(1)}, f32[256,128]{1,0:T(8,128)}, u32[]{:S(2)}) %copy-start.3) | copy-done | bytes 131096
  3.6 0.0 copy-start.4
  3.6 0.7 %copy-done.4 = s32[1,2,4]{2,1,0:T(2,128)S(1)} copy-done((s32[1,2,4]{2,1,0:T(2,128)S(1)}, s32[1,2,4]{2,1,0:T(2,128)}, u32[]{:S(2)}) %copy-start.4) | copy-done | bytes 56
  4.3 0.0 copy-start.5
  4.3 0.7 %copy-done.5 = s32[1,2]{1,0:T(1,128)S(1)} copy-done((s32[1,2]{1,0:T(1,128)S(1)}, s32[1,2]{1,0:T(1,128)}, u32[]{:S(2)}) %copy-start.5) | copy-done | bytes 32
  5.0 41.5 %shard_map.64 = f32[1024,128]{1,0:T(8,128)S(1)} custom-call(f32[256,128]{1,0:T(8,128)S(1)} %copy-done, f32[256,128]{1,0:T(8,128)S(1)} %copy-done.1, f32[256,128]{1,0:T(8,128)S(1)} %copy-done.2, f32[256,128]{1,0:T(8,128)S(1)} %copy-done.3, s32[1,2,4]{2,1,0:T(2,128)S(1)} %copy-done.4, s32[1,2]{1,0:T(1,128)S(1)} %copy-done.5), custom_call_target="tpu_custom_call" | custom-call | tf_op jit(solution)/shard_map/pallas_call | solution.py:317
  46.5 0.8 %copy.8 = f32[1024,128]{1,0:T(8,128)} copy(f32[1024,128]{1,0:T(8,128)S(1)} %shard_map.64) | data formatting | bytes 1048576
Async XLA Ops:
  0.0 0.9 %copy-start = (f32[256,128]{1,0:T(8,128)S(1)}, f32[256,128]{1,0:T(8,128)}, u32[]{:S(2)}) copy-start(f32[256,128]{1,0:T(8,128)} %diag_ref.1) | copy-start | bytes 393220
  0.9 0.9 %copy-start.1 = (f32[256,128]{1,0:T(8,128)S(1)}, f32[256,128]{1,0:T(8,128)}, u32[]{:S(2)}) copy-start(f32[256,128]{1,0:T(8,128)} %near_ref.1) | copy-start | bytes 393220
  1.8 0.9 %copy-start.2 = (f32[256,128]{1,0:T(8,128)S(1)}, f32[256,128]{1,0:T(8,128)}, u32[]{:S(2)}) copy-start(f32[256,128]{1,0:T(8,128)} %far_ref.1) | copy-start | bytes 393220
  2.7 0.9 %copy-start.3 = (f32[256,128]{1,0:T(8,128)S(1)}, f32[256,128]{1,0:T(8,128)}, u32[]{:S(2)}) copy-start(f32[256,128]{1,0:T(8,128)} %leaf_ref.1) | copy-start | bytes 393220
  3.6 0.7 %copy-start.4 = (s32[1,2,4]{2,1,0:T(2,128)S(1)}, s32[1,2,4]{2,1,0:T(2,128)}, u32[]{:S(2)}) copy-start(s32[1,2,4]{2,1,0:T(2,128)} %rows_ref.1) | copy-start | bytes 100
  4.3 0.7 %copy-start.5 = (s32[1,2]{1,0:T(1,128)S(1)}, s32[1,2]{1,0:T(1,128)}, u32[]{:S(2)}) copy-start(s32[1,2]{1,0:T(1,128)} %counts_ref.1) | copy-start | bytes 28
where the time goes:
time: 47.5 us; the launch traced here: 47.3 us
  Pallas kernels  41.5 us (87%)
  local copies, waits for them, and re-layouts  5.74 us (12%)
    pallas_call x1, Pallas kernels, per_device(): pl.pallas_call(functools.partial(kernel, stride), out_shape=jax.ShapeDtyp...  41.5 us
    unnamed x13, local copies, waits for them, and re-layouts  5.74 us

commit v1 on v0

v1 whole, which is shorter than its diff:
```python
import functools

import jax
import jax.numpy as jnp
from jax import lax
from jax.experimental import pallas as pl
from jax.experimental.pallas import tpu as pltpu

MESH = pl.DeviceIdType.MESH
T = 256
H = 128
KP = 96
F32 = jnp.float32
BF16 = jnp.bfloat16


def split(x):
    high = x.astype(BF16)
    return high, (x - high.astype(F32)).astype(BF16)


def nn(a, b):
    return lax.dot_general(a, b, (((1,), (0,)), ((), ())), preferred_element_type=F32)


def nt(a, b):
    return lax.dot_general(a, b, (((1,), (1,)), ((), ())), preferred_element_type=F32)


def mm(a, b, dot=nn):
    rows = a[0].shape[0]
    if rows <= 128:
        both = dot(jnp.concatenate([a[0], a[1]], 0), b[0])
        return both[:rows] + (both[rows:] + dot(a[0], b[1]))
    return dot(a[0], b[0]) + (dot(a[0], b[1]) + dot(a[1], b[0]))


def put(pair_ref, index, value):
    high, low = split(value)
    pair_ref[(0,) + index] = high
    pair_ref[(1,) + index] = low


def get(pair_ref, index):
    return pair_ref[(0,) + index], pair_ref[(1,) + index]


ALL = slice(None)


def tl(k):
    return slice(k * T, (k + 1) * T)


def eye(offset, rows):
    row = lax.broadcasted_iota(jnp.int32, (rows, T), 0) + offset
    col = lax.broadcasted_iota(jnp.int32, (rows, T), 1)
    return jnp.where(row == col, 1.0, 0.0).astype(F32)


def kernel(
    stride,
    diag_ref, near_ref, far_ref, leaf_ref, rows_ref, counts_ref,
    out_ref,
    zin, rows_s, counts_s, own_diag, c_raw, c_own, d_raw, uraw, packed, ncr, masks, mown,
    pf, ff, fx, ut, a_mat, far_s, p_mat, q_mat, f_mat, f_cross,
    local, ssem, rsem,
):
    leaf = lax.axis_index("leaf")
    core = lax.axis_index("tile")
    pos = leaf // stride
    rest = leaf % stride
    pos1 = pos + 1 - 2 * (pos % 2)
    pos2 = (pos + 2) % 4
    pos3 = 3 - pos
    spot = (pos, pos1, pos2, pos3)
    dev1 = (pos1 * stride + rest, core)
    dev3 = (pos3 * stride + rest, core)
    mate = (leaf, 1 - core)
    half = pl.multiple_of(core * H, H)
    mine = pl.ds(half, H)
    away = pl.ds(pl.multiple_of(H - half, H), H)

    barrier = pltpu.get_barrier_semaphore()
    for device in (dev1, dev3, mate):
        pl.semaphore_signal(barrier, inc=1, device_id=device, device_id_type=MESH)

    loads = [
        pltpu.make_async_copy(a, b, local.at[i])
        for i, (a, b) in enumerate((
            (leaf_ref, zin), (near_ref, c_raw.at[0, core]), (diag_ref, own_diag.at[core]),
            (far_ref, d_raw.at[0, core]), (rows_ref, rows_s), (counts_ref, counts_s),
        ))
    ]
    for load in loads:
        load.start()

    copies = {}

    def plan(name, src, dst, device):
        index = len(copies)
        copies[name] = pltpu.make_async_remote_copy(
            src_ref=src, dst_ref=dst, send_sem=ssem.at[index], recv_sem=rsem.at[index],
            device_id=device, device_id_type=MESH,
        )

    def same(name, ref, device):
        plan(name, ref, ref, device)

    def start(*names):
        for name in names:
            copies[name].start()

    def arrived(*names):
        for name in names:
            copies[name].wait_recv()

    plan("C1", c_raw.at[0, core], c_raw.at[1, core], dev1)
    for key, buf, rows in (("U", uraw, 64), ("K", packed, KP), ("D", d_raw, H)):
        first, second = pl.ds(0, rows), pl.ds(rows, rows)
        plan(key + "1b", buf.at[0, core, second], buf.at[1, core, second], dev1)
        plan(key + "1a", buf.at[0, core, first], buf.at[1, core, first], dev1)
        plan(key + "3a", buf.at[0, core, first], buf.at[3, core, first], dev3)
        plan(key + "3b", buf.at[0, core, second], buf.at[3, core, second], dev3)
        plan("f" + key + "1", buf.at[3, core, first], buf.at[2, core, first], dev1)
        plan("f" + key + "3", buf.at[1, core, second], buf.at[2, core, second], dev3)
        if key != "K":
            same("m" + key + "0", buf.at[0, core], mate)
        same("m" + key + "1", buf.at[1, core], mate)
        same("m" + key + "3", buf.at[3, core], mate)
        same("m" + key + "2a", buf.at[2, core, first], mate)
        same("m" + key + "2b", buf.at[2, core, second], mate)
    plan("mC0", c_raw.at[0, core, away], c_own.at[:], mate)
    same("mR", ncr.at[0, mine], mate)
    same("mG0", own_diag.at[core], mate)
    plan("N3", ncr.at[0, mine], ncr.at[1, mine], dev3)
    same("mN", ncr.at[1, mine], mate)
    plan("M1", mown, masks.at[1], dev1)
    plan("M3", mown, masks.at[3], dev3)
    plan("fM1", masks.at[3], masks.at[2], dev1)
    for g in range(2):
        for r in range(2):
            same("xP%d%d" % (g, r), pf.at[g, core, r], mate)
    for g in range(2):
        same("xF%d" % g, ff.at[g, core], mate)
    same("xX", fx.at[core], mate)

    loads[4].wait()
    loads[5].wait()
    for level in range(2):
        for s in range(4):
            hit = jnp.float32(0.0)
            for e in range(4):
                value = rows_s[0, level, e]
                place = 2 * (value // (2 * stride) % 2) + value // stride % 2
                live = jnp.logical_and(e < counts_s[0, level], place == spot[s])
                hit = jnp.where(live, jnp.float32(1.0), hit)
            mown[level * 4 + s:level * 4 + s + 1, :] = jnp.full((1, 128), hit, F32)
    masks[0] = mown[...]

    loads[0].wait()
    uraw[0, core] = zin[...].T
    loads[1].wait()
    pl.semaphore_wait(barrier, 3)
    start("M1", "M3", "C1", "U3a", "U3b", "U1b", "U1a", "mC0", "mU0")
    loads[2].wait()
    packed[0, core, 0:H] = own_diag[core, pl.ds(half, H)]
    other = own_diag[core, pl.ds(pl.multiple_of(H - half, H), H)]
    other = jnp.where(core == 0, other, other.T)
    packed[0, core, H:H + 64] = jnp.where(core == 0, other[0:64], other[64:128])
    start("K3a", "K3b", "K1b", "K1a", "mG0")
    loads[3].wait()
    start("mD0")
    def mask(level, column, row):
        line = masks[column, level * 4 + (column ^ row):level * 4 + (column ^ row) + 1, :]
        return jnp.concatenate([line, line], axis=1)

    def wide(line):
        return jnp.concatenate([line, line], axis=1)

    def whole(ref, slot):
        return jnp.concatenate([ref[slot, 0], ref[slot, 1]], axis=1)

    def put_near(g, cross):
        first, second = (0, 1) if g == 0 else (1, 0)
        put(a_mat, (g, tl(first), tl(second)), cross)
        put(a_mat, (g, tl(second), tl(first)), cross.T)

    def put_diag(slot):
        g, k = slot // 2, slot % 2
        low, high = packed[slot, 0], packed[slot, 1]
        below = jnp.concatenate([low[H:], high[H:]], axis=0)
        full = jnp.concatenate([
            jnp.concatenate([low[:H], below.T], axis=1),
            jnp.concatenate([below, high[:H]], axis=1),
        ], axis=0)
        put(a_mat, (g, tl(k), tl(k)), full)

    def put_leaf(slot):
        put(ut, (slot,), jnp.concatenate([uraw[slot, 0], uraw[slot, 1]], axis=0))

    own_rows = pl.ds(pl.multiple_of(core * T, T), T)
    mate_rows = pl.ds(pl.multiple_of(T - core * T, T), T)

    def sweep1(g, *places):
        hold = {}

        def one():
            for j, r in places:
                hold[j, r] = split(mm(get(ut, (2 * g + j,)), get(a_mat, (g, tl(j), tl(r)))))

        def two():
            for j, r in places:
                f = -0.5 * mm(hold[j, r], get(ut, (2 * g + r,)), nt)
                hold[j, r] = split(f + 1.5 * eye(0, T) if r == j else f)

        def three():
            for j, r in places:
                new = mm(hold[j, r], get(ut, (2 * g + r,)))
                put(p_mat, (g, tl(j), tl(r)), new * mask(0, 2 * g + j, 2 * g + r))

        return one, two, three

    row2 = lax.broadcasted_iota(jnp.int32, (T, 2 * T), 0) + core * T
    col2 = lax.broadcasted_iota(jnp.int32, (T, 2 * T), 1)

    def newton(gram):
        return jnp.where(row2 == col2, 1.5, 0.0) - 0.5 * gram

    def sweep2(g):
        hold = []

        def one():
            hold.append(split(mm(get(p_mat, (g, own_rows)), get(a_mat, (g,)))))

        def two():
            hold.append(split(newton(mm(hold[0], get(p_mat, (g,)), nt))))

        def three():
            for r in range(2):
                line = masks[2 * g + core, pl.ds(core if r == 0 else 1 - core, 1), :]
                new = mm(hold[1], get(p_mat, (g, ALL, tl(r)))) * wide(line)
                pf[g, core, r] = new
                start("xP%d%d" % (g, r))
                put(q_mat, (g, own_rows, tl(r)), new)

        return one, two, three

    def join(g):
        for r in range(2):
            arrived("xP%d%d" % (g, r))
            put(q_mat, (g, mate_rows, tl(r)), pf[g, 1 - core, r])

    def gram1(g):
        hold = []

        def one():
            hold.append(split(mm(get(q_mat, (g, own_rows)), get(a_mat, (g,)))))

        def two():
            f = newton(mm(hold[0], get(q_mat, (g,)), nt))
            ff[g, core] = f
            start("xF%d" % g)
            put(f_mat, (g, own_rows), f)

        return one, two

    def fin(g):
        arrived("xF%d" % g)
        put(f_mat, (g, mate_rows), ff[g, 1 - core])

    def run(*steps):
        for step in steps:
            step()

    arrived("mC0", "C1")
    mixed = c_raw[0, core, mine]
    rows = jnp.where(core == 0, jnp.concatenate([mixed, c_own[...]], axis=1), jnp.concatenate([c_own[...], mixed], axis=1))
    ncr[0, mine] = 0.5 * (rows + c_raw[1, core].T)
    start("N3", "mR")
    arrived("M3")
    start("fM1")
    arrived("U3a")
    start("fU1")
    arrived("U3b")
    start("mU3")
    arrived("K3a")
    start("fK1", "D1b", "D1a")
    arrived("mG0", "mU0")
    put(a_mat, (0, tl(0), tl(0)), jnp.concatenate([own_diag[0], own_diag[1]], axis=1))
    put_leaf(0)
    arrived("U1b")
    start("fU3")
    arrived("U1a", "K3b")
    start("mU1", "mK3")
    arrived("mR", "M1")
    put_near(0, ncr[0])
    run(*sweep1(0, (0, 0)))
    arrived("K1b")
    start("fK3", "D3a", "D3b")
    arrived("mU1")
    put_leaf(1)
    a = sweep1(0, (0, 1), (1, 0))
    run(a[0])
    arrived("K1a")
    start("mK1")
    run(*a[1:])
    arrived("mU3", "mK3")
    put_leaf(3)
    put_diag(3)
    arrived("fM1")
    arrived("N3")
    start("mN")
    arrived("mK1")
    put_diag(1)
    arrived("fU1")
    start("mU2a")
    a, b = sweep1(0, (1, 1)), sweep1(1, (1, 1))
    run(a[0], b[0], a[1], b[1])
    arrived("fU3")
    start("mU2b")
    run(a[2], b[2])
    a = sweep2(0)
    run(a[0])
    arrived("fK1")
    start("mK2a")
    arrived("mN")
    put_near(1, ncr[1])
    run(a[1])
    arrived("fK3")
    start("mK2b")
    arrived("mU2a", "mU2b")
    put_leaf(2)
    b = sweep1(1, (0, 1), (1, 0))
    run(a[2], b[0], b[1])
    arrived("mK2a", "mK2b")
    put_diag(2)
    a = sweep1(1, (0, 0))
    run(a[0], b[2])
    arrived("D1b")
    start("fD3")
    run(a[1])
    arrived("D3a")
    start("fD1")
    join(0)
    run(a[2])
    arrived("D1a", "D3b")
    start("mD1", "mD3")
    a, b = sweep2(1), gram1(0)
    run(a[0], b[0], a[1], b[1], a[2])
    arrived("mD1", "mD3")
    put(far_s, (1,), 0.5 * (whole(d_raw, 1) + whole(d_raw, 3).T))
    arrived("fD1", "fD3")
    start("mD2a", "mD2b")
    fin(0)
    join(1)
    a = gram1(1)
    run(a[0])
    u0 = mm(get(f_mat, (0, mine, ALL)), get(q_mat, (0,)))
    run(a[1])
    arrived("mD0", "mD2a", "mD2b")
    put(far_s, (0,), 0.5 * (whole(d_raw, 0) + whole(d_raw, 2).T))

    second = pl.ds(pl.multiple_of(T + half, H), H)
    v = []
    for k in range(2):
        rows = tuple(
            jnp.concatenate([q_mat[i, 0, mine, tl(k)], q_mat[i, 0, second, tl(k)]], axis=0)
            for i in range(2)
        )
        v.append(mm(rows, get(far_s, (k,))))
    f = -0.5 * mm(split(jnp.concatenate(v, axis=1)), get(q_mat, (1,)), nt)
    fx[core] = f
    start("xX")
    f = split(f)
    for i in range(2):
        f_cross[i, mine] = f[i][:H]
        f_cross[i, second] = f[i][H:]
    u1 = mm((f[0][:H], f[1][:H]), get(q_mat, (1,)))
    u = [u0[:, tl(0)], u0[:, tl(1)], u1[:, tl(0)], u1[:, tl(1)]]
    u = [u[r] * mask(1, 0, r) for r in range(4)]
    us = [split(x) for x in u]

    def beside(parts):
        return tuple(jnp.concatenate([part[i] for part in parts], axis=1) for i in range(2))

    v = []
    for g in range(2):
        vg = mm(beside(us[2 * g:2 * g + 2]), get(a_mat, (g,)))
        for k in range(2):
            extra = mm(us[2 - 2 * g + k], get(far_s, (k,)), nn if g == 1 else nt)
            v.append(split(vg[:, tl(k)] + extra))
    ga = [mm(v[r], get(q_mat, (r // 2, ALL, tl(r % 2))), nt) for r in range(4)]
    fin(1)
    arrived("xX")
    f = split(fx[1 - core])
    for i in range(2):
        f_cross[i, away] = f[i][:H]
        f_cross[i, pl.ds(pl.multiple_of(T + H - half, H), H)] = f[i][H:]
    ds = []
    for l in range(4):
        lhs = []
        for g in range(2):
            m0, m1 = wide(mask(1, l, 2 * g)), wide(mask(1, l, 2 * g + 1))
            lhs.append(split(m0 * ga[2 * g] + m1 * ga[2 * g + 1]))
        k = l % 2
        if l < 2:
            gram = mm(lhs[0], get(f_mat, (0, ALL, tl(k)))) + mm(lhs[1], get(f_cross, (tl(k), ALL)), nt)
        else:
            gram = mm(lhs[0], get(f_cross, (ALL, tl(k)))) + mm(lhs[1], get(f_mat, (1, ALL, tl(k))))
        ds.append(split(eye(half, H) - gram if l == 0 else -gram))
    terms = [[], []]
    for l in range(4):
        k = l % 2
        if l < 2:
            terms[0].append(mm(ds[l], get(f_mat, (0, tl(k), ALL))))
            terms[1].append(mm(ds[l], get(f_cross, (tl(k), ALL))))
        else:
            terms[0].append(mm(ds[l], get(f_cross, (ALL, tl(k))), nt))
            terms[1].append(mm(ds[l], get(f_mat, (1, tl(k), ALL))))
    for r in range(4):
        g, k = r // 2, r % 2
        x = 0.0
        for l in range(4):
            x = x + wide(mask(1, l, r)) * terms[g][l]
        last = u[r] + 0.5 * mm(split(x), get(q_mat, (g, ALL, tl(k))))
        last = last * mask(1, 0, r)
        out_ref[pl.ds(pl.multiple_of(spot[r] * T, T), T), :] = last.T

    for copy in copies.values():
        copy.wait_send()


def per_device(margin_diag, coupling_near, coupling_far, leaf_factor, tile_rows, tile_counts):
    stride = lax.axis_size("leaf") // 4
    vmem = pl.BlockSpec(memory_space=pltpu.VMEM)
    hbm = pl.BlockSpec(memory_space=pl.ANY)
    dma = pltpu.SemaphoreType.DMA
    return pl.pallas_call(
        functools.partial(kernel, stride),
        out_shape=jax.ShapeDtypeStruct((4 * T, H), F32),
        in_specs=[hbm] * 6,
        out_specs=vmem,
        scratch_shapes=[
            pltpu.VMEM((T, H), F32),
            pltpu.SMEM((1, 2, 4), jnp.int32),
            pltpu.SMEM((1, 2), jnp.int32),
            pltpu.VMEM((2, T, H), F32),
            pltpu.VMEM((2, 2, T, H), F32),
            pltpu.VMEM((H, H), F32),
            pltpu.VMEM((4, 2, T, H), F32),
            pltpu.VMEM((4, 2, H, T), F32),
            pltpu.VMEM((4, 2, 2 * KP, H), F32),
            pltpu.VMEM((2, T, T), F32),
            pltpu.VMEM((4, 8, 128), F32),
            pltpu.VMEM((8, 128), F32),
            pltpu.VMEM((2, 2, 2, T, T), F32),
            pltpu.VMEM((2, 2, T, 2 * T), F32),
            pltpu.VMEM((2, T, 2 * T), F32),
            pltpu.VMEM((2, 4, T, T), BF16),
            pltpu.VMEM((2, 2, 2 * T, 2 * T), BF16),
            pltpu.VMEM((2, 2, T, T), BF16),
            pltpu.VMEM((2, 2, 2 * T, 2 * T), BF16),
            pltpu.VMEM((2, 2, 2 * T, 2 * T), BF16),
            pltpu.VMEM((2, 2, 2 * T, 2 * T), BF16),
            pltpu.VMEM((2, 2 * T, 2 * T), BF16),
            dma((6,)), dma((64,)), dma((64,)),
        ],
        compiler_params=pltpu.CompilerParams(
            collective_id=0, has_side_effects=True, vmem_limit_bytes=50 * 2**20
        ),
    )(*[pltpu.with_memory_space_constraint(x, pltpu.HBM) for x in (margin_diag, coupling_near, coupling_far, leaf_factor, tile_rows, tile_counts)])


def solution(mesh):
    spec = jax.sharding.PartitionSpec
    return jax.shard_map(
        per_device,
        mesh=mesh,
        in_specs=(
            spec("leaf", "tile"),
            spec("leaf", "tile"),
            spec("leaf", "tile"),
            spec("leaf", "tile"),
            spec("leaf", None, None),
            spec("leaf", None),
        ),
        out_specs=spec(None, ("leaf", "tile")),
        check_vma=False,
    )
```

time: 47.5 us -> 39.2 us (0.83)
  the two profiles are of different devices: /device:TPU:3 before, /device:TPU:1 now
where the time goes in v1:
time: 39.2 us; the launch traced here: 39.1 us
  Pallas kernels  38.3 us (98%)
  local copies, waits for them, and re-layouts  0.8 us (2%)
    pallas_call x1, Pallas kernels, per_device(): pl.pallas_call(functools.partial(kernel, stride), out_shape=jax.ShapeDtyp...  38.3 us
    unnamed x1, local copies, waits for them, and re-layouts  0.8 us

profile of v1, /device:TPU:1, one launch (start us, length us, event | category | flops | bytes accessed | tf_op | source)
XLA Modules:
  0.0 39.1 jit_solution(7139851539635254847)
XLA Ops:
  0.0 38.3 %shard_map.64 = f32[1024,128]{1,0:T(8,128)S(1)} custom-call(f32[256,128]{1,0:T(8,128)} %diag_ref.1, f32[256,128]{1,0:T(8,128)} %near_ref.1, f32[256,128]{1,0:T(8,128)} %far_ref.1, f32[256,128]{1,0:T(8,128)} %leaf_ref.1, s32[1,2,4]{2,1,0:T(2,128)} %rows_ref.1, s32[1,2]{1,0:T(1,128)} %counts_ref.1), custom_call_target="tpu_custom_call" | custom-call | tf_op jit(solution)/shard_map/pallas_call | solution.py:439
  38.3 0.8 %copy.8 = f32[1024,128]{1,0:T(8,128)} copy(f32[1024,128]{1,0:T(8,128)S(1)} %shard_map.64) | data formatting | bytes 1048576

commit v2 on v1

--- a/solution.py
+++ b/solution.py
@@ -9,7 +9,8 @@
 MESH = pl.DeviceIdType.MESH
 T = 256
 H = 128
-KP = 96
+Q = 64
+KP = 136
 F32 = jnp.float32
 BF16 = jnp.bfloat16
 
@@ -58,12 +59,32 @@
     return jnp.where(row == col, 1.0, 0.0).astype(F32)
 
 
+def fold(block):
+    row = lax.broadcasted_iota(jnp.int32, (Q, H), 0)
+    col = lax.broadcasted_iota(jnp.int32, (Q, H), 1)
+    top, low = block[:Q], block[Q:]
+    inside = jnp.logical_and(col > row, col < Q)
+    line = jnp.sum(jnp.where(col == row + Q, low, 0.0), axis=0, keepdims=True)
+    return jnp.concatenate([jnp.where(inside, pltpu.roll(low, Q, 1), top), jnp.broadcast_to(line, (8, H))], axis=0)
+
+
+def unfold(rows):
+    row = lax.broadcasted_iota(jnp.int32, (Q, H), 0)
+    col = lax.broadcasted_iota(jnp.int32, (Q, H), 1)
+    top, line = rows[:Q], rows[Q:Q + 1]
+    upper = jnp.where(jnp.logical_or(col < row, col >= Q), top, 0.0)
+    lower = jnp.where(col > row + Q, pltpu.roll(top, Q, 1), 0.0)
+    side = jnp.concatenate([upper, lower], axis=0)
+    diagonal = jnp.concatenate([jnp.where(col == row, top, 0.0), jnp.where(col == row + Q, line, 0.0)], axis=0)
+    return side + side.T + diagonal
+
+
 def kernel(
     stride,
     diag_ref, near_ref, far_ref, leaf_ref, rows_ref, counts_ref,
     out_ref,
     zin, rows_s, counts_s, own_diag, c_raw, c_own, d_raw, uraw, packed, ncr, masks, mown,
-    pf, ff, fx, ut, a_mat, far_s, p_mat, q_mat, f_mat, f_cross,
+    unit, pf, ff, fx, ut, a_mat, far_s, p_mat, q_mat, f_mat, f_cross,
     local, ssem, rsem,
 ):
     leaf = lax.axis_index("leaf")
@@ -116,8 +137,8 @@
             copies[name].wait_recv()
 
     plan("C1", c_raw.at[0, core], c_raw.at[1, core], dev1)
-    for key, buf, rows in (("U", uraw, 64), ("K", packed, KP), ("D", d_raw, H)):
-        first, second = pl.ds(0, rows), pl.ds(rows, rows)
+    for key, buf, rows in (("U", uraw, (Q, Q)), ("K", packed, (KP - Q, Q)), ("D", d_raw, (H, H))):
+        first, second = pl.ds(0, rows[0]), pl.ds(rows[0], rows[1])
         plan(key + "1b", buf.at[0, core, second], buf.at[1, core, second], dev1)
         plan(key + "1a", buf.at[0, core, first], buf.at[1, core, first], dev1)
         plan(key + "3a", buf.at[0, core, first], buf.at[3, core, first], dev3)
@@ -158,16 +179,21 @@
             mown[level * 4 + s:level * 4 + s + 1, :] = jnp.full((1, 128), hit, F32)
     masks[0] = mown[...]
 
+    unit[0, :, :T] = 1.5 * eye(0, T)
+    unit[0, :, T:] = jnp.zeros((T, T), F32)
+    unit[1, :, :T] = jnp.zeros((T, T), F32)
+    unit[1, :, T:] = 1.5 * eye(0, T)
     loads[0].wait()
     uraw[0, core] = zin[...].T
     loads[1].wait()
     pl.semaphore_wait(barrier, 3)
     start("M1", "M3", "C1", "U3a", "U3b", "U1b", "U1a", "mC0", "mU0")
     loads[2].wait()
-    packed[0, core, 0:H] = own_diag[core, pl.ds(half, H)]
-    other = own_diag[core, pl.ds(pl.multiple_of(H - half, H), H)]
+    top = own_diag[core, mine]
+    packed[0, core, 0:KP - Q] = fold(top)
+    other = own_diag[core, away]
     other = jnp.where(core == 0, other, other.T)
-    packed[0, core, H:H + 64] = jnp.where(core == 0, other[0:64], other[64:128])
+    packed[0, core, KP - Q:KP] = jnp.where(core == 0, other[:Q], other[Q:])
     start("K3a", "K3b", "K1b", "K1a", "mG0")
     loads[3].wait()
     start("mD0")
@@ -189,12 +215,12 @@
     def put_diag(slot):
         g, k = slot // 2, slot % 2
         low, high = packed[slot, 0], packed[slot, 1]
-        below = jnp.concatenate([low[H:], high[H:]], axis=0)
+        below = jnp.concatenate([low[KP - Q:], high[KP - Q:]], axis=0)
         full = jnp.concatenate([
-            jnp.concatenate([low[:H], below.T], axis=1),
-            jnp.concatenate([below, high[:H]], axis=1),
+            jnp.concatenate([unfold(low), below.T], axis=1),
+            jnp.concatenate([below, unfold(high)], axis=1),
         ], axis=0)
-        put(a_mat, (g, tl(k), tl(k)), full)
+        put(a_mat, (g, tl(k), tl(k)), -0.5 * full)
 
     def put_leaf(slot):
         put(ut, (slot,), jnp.concatenate([uraw[slot, 0], uraw[slot, 1]], axis=0))
@@ -211,8 +237,8 @@
 
         def two():
             for j, r in places:
-                f = -0.5 * mm(hold[j, r], get(ut, (2 * g + r,)), nt)
-                hold[j, r] = split(f + 1.5 * eye(0, T) if r == j else f)
+                f = mm(hold[j, r], get(ut, (2 * g + r,)), nt)
+                hold[j, r] = split(f + unit[0, :, :T] if r == j else f)
 
         def three():
             for j, r in places:
@@ -221,11 +247,8 @@
 
         return one, two, three
 
-    row2 = lax.broadcasted_iota(jnp.int32, (T, 2 * T), 0) + core * T
-    col2 = lax.broadcasted_iota(jnp.int32, (T, 2 * T), 1)
-
     def newton(gram):
-        return jnp.where(row2 == col2, 1.5, 0.0) - 0.5 * gram
+        return gram + unit[core]
 
     def sweep2(g):
         hold = []
@@ -241,14 +264,13 @@
                 line = masks[2 * g + core, pl.ds(core if r == 0 else 1 - core, 1), :]
                 new = mm(hold[1], get(p_mat, (g, ALL, tl(r)))) * wide(line)
                 pf[g, core, r] = new
-                start("xP%d%d" % (g, r))
                 put(q_mat, (g, own_rows, tl(r)), new)
+            start("xP%d0" % g, "xP%d1" % g)
 
         return one, two, three
 
     def join(g):
         for r in range(2):
-            arrived("xP%d%d" % (g, r))
             put(q_mat, (g, mate_rows, tl(r)), pf[g, 1 - core, r])
 
     def gram1(g):
@@ -266,7 +288,6 @@
         return one, two
 
     def fin(g):
-        arrived("xF%d" % g)
         put(f_mat, (g, mate_rows), ff[g, 1 - core])
 
     def run(*steps):
@@ -276,7 +297,7 @@
     arrived("mC0", "C1")
     mixed = c_raw[0, core, mine]
     rows = jnp.where(core == 0, jnp.concatenate([mixed, c_own[...]], axis=1), jnp.concatenate([c_own[...], mixed], axis=1))
-    ncr[0, mine] = 0.5 * (rows + c_raw[1, core].T)
+    ncr[0, mine] = -0.25 * (rows + c_raw[1, core].T)
     start("N3", "mR")
     arrived("M3")
     start("fM1")
@@ -286,80 +307,67 @@
     start("mU3")
     arrived("K3a")
     start("fK1", "D1b", "D1a")
-    arrived("mG0", "mU0")
-    put(a_mat, (0, tl(0), tl(0)), jnp.concatenate([own_diag[0], own_diag[1]], axis=1))
-    put_leaf(0)
     arrived("U1b")
     start("fU3")
+    arrived("mG0", "mU0", "mR", "M1")
+    put(a_mat, (0, tl(0), tl(0)), -0.5 * jnp.concatenate([own_diag[0], own_diag[1]], axis=1))
+    put_leaf(0)
+    put_near(0, ncr[0])
+    run(*sweep1(0, (0, 0)))
     arrived("U1a", "K3b")
     start("mU1", "mK3")
-    arrived("mR", "M1")
-    put_near(0, ncr[0])
-    run(*sweep1(0, (0, 0)))
     arrived("K1b")
     start("fK3", "D3a", "D3b")
     arrived("mU1")
     put_leaf(1)
     a = sweep1(0, (0, 1), (1, 0))
     run(a[0])
-    arrived("K1a")
+    arrived("K1a", "mU3", "mK3")
     start("mK1")
-    run(*a[1:])
-    arrived("mU3", "mK3")
     put_leaf(3)
     put_diag(3)
-    arrived("fM1")
-    arrived("N3")
-    start("mN")
-    arrived("mK1")
+    run(*a[1:])
+    b = sweep1(1, (1, 1))
+    run(b[0])
+    arrived("fM1", "N3", "mK1", "fU1")
+    start("mN", "mU2a")
     put_diag(1)
-    arrived("fU1")
-    start("mU2a")
-    a, b = sweep1(0, (1, 1)), sweep1(1, (1, 1))
-    run(a[0], b[0], a[1], b[1])
-    arrived("fU3")
-    start("mU2b")
-    run(a[2], b[2])
+    a = sweep1(0, (1, 1))
+    run(a[0], b[1], a[1], b[2], a[2])
+    arrived("fU3", "fK1")
+    start("mU2b", "mK2a")
     a = sweep2(0)
-    run(a[0])
-    arrived("fK1")
-    start("mK2a")
-    arrived("mN")
+    run(a[0], a[1])
+    arrived("fK3", "mN", "mU2a", "mU2b")
+    start("mK2b")
     put_near(1, ncr[1])
-    run(a[1])
-    arrived("fK3")
-    start("mK2b")
-    arrived("mU2a", "mU2b")
     put_leaf(2)
     b = sweep1(1, (0, 1), (1, 0))
-    run(a[2], b[0], b[1])
+    run(a[2])
+    arrived("D1b", "D3a")
+    start("fD3", "fD1")
+    run(*b)
     arrived("mK2a", "mK2b")
     put_diag(2)
-    a = sweep1(1, (0, 0))
-    run(a[0], b[2])
-    arrived("D1b")
-    start("fD3")
-    run(a[1])
-    arrived("D3a")
-    start("fD1")
-    join(0)
-    run(a[2])
+    run(*sweep1(1, (0, 0)))
     arrived("D1a", "D3b")
     start("mD1", "mD3")
-    a, b = sweep2(1), gram1(0)
-    run(a[0], b[0], a[1], b[1], a[2])
-    arrived("mD1", "mD3")
-    put(far_s, (1,), 0.5 * (whole(d_raw, 1) + whole(d_raw, 3).T))
-    arrived("fD1", "fD3")
+    run(*sweep2(1))
+    arrived("xP00", "xP01")
+    join(0)
+    a = gram1(0)
+    run(a[0])
+    arrived("mD1", "mD3", "fD1", "fD3")
     start("mD2a", "mD2b")
+    put(far_s, (1,), -0.25 * (whole(d_raw, 1) + whole(d_raw, 3).T))
+    run(a[1])
+    arrived("xP10", "xP11")
+    join(1)
+    run(*gram1(1))
+    arrived("xF0", "mD0", "mD2a", "mD2b")
     fin(0)
-    join(1)
-    a = gram1(1)
-    run(a[0])
     u0 = mm(get(f_mat, (0, mine, ALL)), get(q_mat, (0,)))
-    run(a[1])
-    arrived("mD0", "mD2a", "mD2b")
-    put(far_s, (0,), 0.5 * (whole(d_raw, 0) + whole(d_raw, 2).T))
+    put(far_s, (0,), -0.25 * (whole(d_raw, 0) + whole(d_raw, 2).T))
 
     second = pl.ds(pl.multiple_of(T + half, H), H)
     v = []
@@ -369,7 +377,7 @@
             for i in range(2)
         )
         v.append(mm(rows, get(far_s, (k,))))
-    f = -0.5 * mm(split(jnp.concatenate(v, axis=1)), get(q_mat, (1,)), nt)
+    f = mm(split(jnp.concatenate(v, axis=1)), get(q_mat, (1,)), nt)
     fx[core] = f
     start("xX")
     f = split(f)
@@ -391,8 +399,8 @@
             extra = mm(us[2 - 2 * g + k], get(far_s, (k,)), nn if g == 1 else nt)
             v.append(split(vg[:, tl(k)] + extra))
     ga = [mm(v[r], get(q_mat, (r // 2, ALL, tl(r % 2))), nt) for r in range(4)]
+    arrived("xF1", "xX")
     fin(1)
-    arrived("xX")
     f = split(fx[1 - core])
     for i in range(2):
         f_cross[i, away] = f[i][:H]
@@ -408,7 +416,7 @@
             gram = mm(lhs[0], get(f_mat, (0, ALL, tl(k)))) + mm(lhs[1], get(f_cross, (tl(k), ALL)), nt)
         else:
             gram = mm(lhs[0], get(f_cross, (ALL, tl(k)))) + mm(lhs[1], get(f_mat, (1, ALL, tl(k))))
-        ds.append(split(eye(half, H) - gram if l == 0 else -gram))
+        ds.append(split(gram + 0.5 * eye(half, H) if l == 0 else gram))
     terms = [[], []]
     for l in range(4):
         k = l % 2
@@ -423,7 +431,7 @@
         x = 0.0
         for l in range(4):
             x = x + wide(mask(1, l, r)) * terms[g][l]
-        last = u[r] + 0.5 * mm(split(x), get(q_mat, (g, ALL, tl(k))))
+        last = u[r] + mm(split(x), get(q_mat, (g, ALL, tl(k))))
         last = last * mask(1, 0, r)
         out_ref[pl.ds(pl.multiple_of(spot[r] * T, T), T), :] = last.T
 
@@ -450,10 +458,11 @@
             pltpu.VMEM((H, H), F32),
             pltpu.VMEM((4, 2, T, H), F32),
             pltpu.VMEM((4, 2, H, T), F32),
-            pltpu.VMEM((4, 2, 2 * KP, H), F32),
+            pltpu.VMEM((4, 2, KP, H), F32),
             pltpu.VMEM((2, T, T), F32),
             pltpu.VMEM((4, 8, 128), F32),
             pltpu.VMEM((8, 128), F32),
+            pltpu.VMEM((2, T, 2 * T), F32),
             pltpu.VMEM((2, 2, 2, T, T), F32),
             pltpu.VMEM((2, 2, T, 2 * T), F32),
             pltpu.VMEM((2, T, 2 * T), F32),

time: 39.2 us -> 37.8 us (0.964)
  Pallas kernels: 38.3 us -> 36.9 us
    pallas_call x1, Pallas kernels: 38.3 us -> 36.9 us  [per_device(): pl.pallas_call(functools.partial(kernel, stride), out_shape=jax.ShapeDtyp...]
where the time goes in v2:
time: 37.8 us; the launch traced here: 37.7 us
  Pallas kernels  36.9 us (98%)
  local copies, waits for them, and re-layouts  0.8 us (2%)
    pallas_call x1, Pallas kernels, per_device(): pl.pallas_call(functools.partial(kernel, stride), out_shape=jax.ShapeDtyp...  36.9 us
    unnamed x1, local copies, waits for them, and re-layouts  0.8 us

profile of v2, /device:TPU:1, one launch (start us, length us, event | category | flops | bytes accessed | tf_op | source)
XLA Modules:
  0.0 37.7 jit_solution(8096896571665454697)
XLA Ops:
  0.0 36.9 %shard_map.64 = f32[1024,128]{1,0:T(8,128)S(1)} custom-call(f32[256,128]{1,0:T(8,128)} %diag_ref.1, f32[256,128]{1,0:T(8,128)} %near_ref.1, f32[256,128]{1,0:T(8,128)} %far_ref.1, f32[256,128]{1,0:T(8,128)} %leaf_ref.1, s32[1,2,4]{2,1,0:T(2,128)} %rows_ref.1, s32[1,2]{1,0:T(1,128)} %counts_ref.1), custom_call_target="tpu_custom_call" | custom-call | tf_op jit(solution)/shard_map/pallas_call | solution.py:447
  36.9 0.8 %copy.8 = f32[1024,128]{1,0:T(8,128)} copy(f32[1024,128]{1,0:T(8,128)S(1)} %shard_map.64) | data formatting | bytes 1048576

commit v3 on v2

--- a/solution.py
+++ b/solution.py
@@ -338,18 +338,19 @@
     start("mU2b", "mK2a")
     a = sweep2(0)
     run(a[0], a[1])
-    arrived("fK3", "mN", "mU2a", "mU2b")
+    arrived("fK3")
     start("mK2b")
+    run(a[2])
+    arrived("mN", "mU2a", "mU2b", "D1b", "D3a")
+    start("fD3", "fD1")
     put_near(1, ncr[1])
     put_leaf(2)
     b = sweep1(1, (0, 1), (1, 0))
-    run(a[2])
-    arrived("D1b", "D3a")
-    start("fD3", "fD1")
-    run(*b)
+    run(b[0])
     arrived("mK2a", "mK2b")
     put_diag(2)
-    run(*sweep1(1, (0, 0)))
+    c = sweep1(1, (0, 0))
+    run(b[1], c[0], b[2], c[1], c[2])
     arrived("D1a", "D3b")
     start("mD1", "mD3")
     run(*sweep2(1))

time: 37.8 us -> 37.1 us (0.981)
  Pallas kernels: 36.9 us -> 36.1 us
    pallas_call x1, Pallas kernels: 36.9 us -> 36.1 us  [per_device(): pl.pallas_call(functools.partial(kernel, stride), out_shape=jax.ShapeDtyp...]
where the time goes in v3:
time: 37.1 us; the launch traced here: 36.9 us
  Pallas kernels  36.1 us (97%)
  local copies, waits for them, and re-layouts  0.8 us (2%)
    pallas_call x1, Pallas kernels, per_device(): pl.pallas_call(functools.partial(kernel, stride), out_shape=jax.ShapeDtyp...  36.1 us
    unnamed x1, local copies, waits for them, and re-layouts  0.8 us

profile of v3, /device:TPU:1, one launch (start us, length us, event | category | flops | bytes accessed | tf_op | source)
XLA Modules:
  0.0 36.9 jit_solution(1880716036884643439)
XLA Ops:
  0.0 36.1 %shard_map.64 = f32[1024,128]{1,0:T(8,128)S(1)} custom-call(f32[256,128]{1,0:T(8,128)} %diag_ref.1, f32[256,128]{1,0:T(8,128)} %near_ref.1, f32[256,128]{1,0:T(8,128)} %far_ref.1, f32[256,128]{1,0:T(8,128)} %leaf_ref.1, s32[1,2,4]{2,1,0:T(2,128)} %rows_ref.1, s32[1,2]{1,0:T(1,128)} %counts_ref.1), custom_call_target="tpu_custom_call" | custom-call | tf_op jit(solution)/shard_map/pallas_call | solution.py:448
  36.1 0.8 %copy.8 = f32[1024,128]{1,0:T(8,128)} copy(f32[1024,128]{1,0:T(8,128)S(1)} %shard_map.64) | data formatting | bytes 1048576
